TPU v7x, 32 devices: a whole 2x2x4 slice. The times are simulated.
32 devices in a mesh: blk: 8 (over z, y), rank: 4 (over x, core).
Axes of the slice: x: 2, y: 2, z: 4, core: 2. Of those that a mesh axis runs over, the one named last changes fastest.
Arguments:
- user_factors: float32 [256, 4096], P('rank', 'blk'), may hold values from -1.5 to 1.5
- item_factors: float32 [256, 8192], P('rank', 'blk'), may hold values from -1.5 to 1.5
- tile_rows: int32 [8, 4, 4096], P('blk'), may hold values from 0 to 511
- tile_cols: int32 [8, 4, 4096], P('blk'), may hold values from 0 to 1023
- tile_vals: float32 [8, 4, 4096], P('blk'), may hold values from -4 to 4
- tile_count: int32 [8, 4], P('blk'), may hold values from 512 to 4096, as said below
Outputs:
- new_users: float32 [256, 4096], P('rank', 'blk')
- new_items: float32 [256, 8192], P('rank', 'blk')
Inputs may be any that keep to these rules, and one draw needn't show every extreme that they name: `tile_count`: in every stratum some block's tile is full (4096 live slots).
All inputs are finite; a program needn't handle non-finite values.
Results may differ from a plain program's by a relative error of at most 0.0003.
Values sent between devices are 32-bit elements; how exact they have to be, the bound alone decides.
A program may use at most 64 MiB of HBM per device.

v0:
```python
import jax
import jax.numpy as jnp
from jax import lax
from jax.sharding import PartitionSpec as P

BATCH = 1024
STRATA = 4


LEARN_RATE = 0.05
DECAY_WEIGHT = 0.02


def shifted(block, axis, distance):
    devices = range(lax.axis_size(axis))
    route = [((i - distance) % len(devices), i) for i in devices]
    return lax.ppermute(block, axis, route)


def rank_total(partial_values):
    return lax.psum(partial_values, "rank")


def selector(indices, count):
    places = jnp.arange(count, dtype=jnp.int32)[:, None]
    return (places == indices[None, :]).astype(jnp.float32)


def pick_columns(block, chooser):
    return jnp.dot(
        block, chooser, preferred_element_type=jnp.float32, precision=lax.Precision.HIGHEST
    )


def spread_columns(steps, chooser):
    return lax.dot_general(
        steps,
        chooser,
        (((1,), (1,)), ((), ())),
        preferred_element_type=jnp.float32,
        precision=lax.Precision.HIGHEST,
    )


def sweep_tile(user_block, item_block, row_index, col_index, rating_vals, live_count, combiner):
    user_count = user_block.shape[1]
    item_count = item_block.shape[1]

    def update(batch_index, carry):
        user_now, item_now = carry
        offset = (batch_index * BATCH).astype(jnp.int32)
        user_rows = lax.dynamic_slice_in_dim(row_index, offset, BATCH)
        item_rows = lax.dynamic_slice_in_dim(col_index, offset, BATCH)
        targets = lax.dynamic_slice_in_dim(rating_vals, offset, BATCH)
        positions = offset + jnp.arange(BATCH, dtype=jnp.int32)
        weights = (positions < live_count).astype(jnp.float32)
        user_pick = selector(user_rows, user_count)
        item_pick = selector(item_rows, item_count)
        user_vecs = pick_columns(user_now, user_pick)
        item_vecs = pick_columns(item_now, item_pick)
        predicted = combiner(jnp.sum(user_vecs * item_vecs, axis=0))
        errors = weights * (targets - predicted)
        user_step = LEARN_RATE * (
            errors[None, :] * item_vecs - DECAY_WEIGHT * weights[None, :] * user_vecs
        )
        item_step = LEARN_RATE * (
            errors[None, :] * user_vecs - DECAY_WEIGHT * weights[None, :] * item_vecs
        )
        return (
            user_now + spread_columns(user_step, user_pick),
            item_now + spread_columns(item_step, item_pick),
        )

    return lax.fori_loop(0, row_index.shape[0] // BATCH, update, (user_block, item_block))


def per_device(user_factors, item_factors, tile_rows, tile_cols, tile_vals, tile_count):
    user_block = user_factors
    item_block = item_factors
    for stratum in range(STRATA):
        if stratum > 0:
            item_block = shifted(item_block, "blk", 1)
        user_block, item_block = sweep_tile(
            user_block,
            item_block,
            tile_rows[0, stratum],
            tile_cols[0, stratum],
            tile_vals[0, stratum],
            tile_count[0, stratum],
            rank_total,
        )
    item_block = shifted(item_block, "blk", 1 - STRATA)
    return (user_block, item_block)


def solution(mesh):
    placed = (
        P("rank", "blk"),
        P("rank", "blk"),
        P("blk", None, None),
        P("blk", None, None),
        P("blk", None, None),
        P("blk", None),
    )
    return jax.shard_map(
        per_device,
        mesh=mesh,
        in_specs=placed,
        out_specs=(P("rank", "blk"), P("rank", "blk")),
        check_vma=False,
    )
```

profile of v0, /device:TPU:0, one launch (start us, length us, event | category | flops | bytes accessed | tf_op | source)
XLA Modules:
  0.0 258.6 jit_solution(12740042411596117091)
XLA Ops:
  2.2 55.0 %while.60 = (s32[]{:T(128)}, f32[64,512]{1,0:T(8,128)S(1)}, f32[64,1024]{1,0:T(8,128)S(1)}, s32[]{:T(128)}, f32[4096]{0:T(1024)S(1)}, /*index=5*/s32[4096]{0:T(1...) while((s32[]{:T(128)}, f32[64,512]{1,0:T(8,128)S(1)}, ...), condition=%wide.region_3.0_spmd, body=%wide.region_0.0_spmd.sunk | while | flops 2419825664 | bytes 3092663 | solution.py:74
  5.4 8.3 %psum.48 = f32[1024]{0:T(1024)S(1)} all-reduce(f32[1024]{0:T(1024)S(1)} %get-tuple-element.750), channel_id=1, replica_groups=mesh['blk'=8,'rank'=4] {'rank'}, use_global_device_ids=true, to_apply=%region_2.0 | all-reduce | flops 1024 | bytes 8192 | tf_op jit(solution)/shard_map/while/body/eval_jaxpr/psum | solution.py:21
  21.1 5.8 %psum.48 = f32[1024]{0:T(1024)S(1)} all-reduce(f32[1024]{0:T(1024)S(1)} %get-tuple-element.750), channel_id=1, replica_groups=mesh['blk'=8,'rank'=4] {'rank'}, use_global_device_ids=true, to_apply=%region_2.0 | all-reduce | flops 1024 | bytes 8192 | tf_op jit(solution)/shard_map/while/body/eval_jaxpr/psum | solution.py:21
  34.2 5.8 %psum.48 = f32[1024]{0:T(1024)S(1)} all-reduce(f32[1024]{0:T(1024)S(1)} %get-tuple-element.750), channel_id=1, replica_groups=mesh['blk'=8,'rank'=4] {'rank'}, use_global_device_ids=true, to_apply=%region_2.0 | all-reduce | flops 1024 | bytes 8192 | tf_op jit(solution)/shard_map/while/body/eval_jaxpr/psum | solution.py:21
  47.4 5.7 %psum.48 = f32[1024]{0:T(1024)S(1)} all-reduce(f32[1024]{0:T(1024)S(1)} %get-tuple-element.750), channel_id=1, replica_groups=mesh['blk'=8,'rank'=4] {'rank'}, use_global_device_ids=true, to_apply=%region_2.0 | all-reduce | flops 1024 | bytes 8192 | tf_op jit(solution)/shard_map/while/body/eval_jaxpr/psum | solution.py:21
  58.9 9.4 %collective-permute-done = f32[64,1024]{1,0:T(8,128)S(1)} collective-permute-done((f32[64,1024]{1,0:T(8,128)S(1)}, f32[64,1024]{1,0:T(8,128)S(1)}, u32[]{:S(2)}, u32[]{:S(2)}) %collective-permute-start) | collective-permute-done | bytes 262176 | tf_op jit(solution)/shard_map/ppermute | solution.py:17
  68.3 53.0 %while.61 = (s32[]{:T(128)}, f32[64,512]{1,0:T(8,128)S(1)}, f32[64,1024]{1,0:T(8,128)S(1)}, s32[]{:T(128)}, f32[4096]{0:T(1024)S(1)}, /*index=5*/s32[4096]{0:T(1...) while((s32[]{:T(128)}, f32[64,512]{1,0:T(8,128)S(1)}, ...), condition=%wide.region_7.0_spmd, body=%wide.region_4.0_spmd.sunk | while | flops 2419825664 | bytes 3092663 | solution.py:74
  71.3 5.7 %psum.49 = f32[1024]{0:T(1024)S(1)} all-reduce(f32[1024]{0:T(1024)S(1)} %get-tuple-element.759), channel_id=1, replica_groups=mesh['blk'=8,'rank'=4] {'rank'}, use_global_device_ids=true, to_apply=%region_6.0 | all-reduce | flops 1024 | bytes 8192 | tf_op jit(solution)/shard_map/while/body/eval_jaxpr/psum | solution.py:21
  84.3 6.6 %psum.49 = f32[1024]{0:T(1024)S(1)} all-reduce(f32[1024]{0:T(1024)S(1)} %get-tuple-element.759), channel_id=1, replica_groups=mesh['blk'=8,'rank'=4] {'rank'}, use_global_device_ids=true, to_apply=%region_6.0 | all-reduce | flops 1024 | bytes 8192 | tf_op jit(solution)/shard_map/while/body/eval_jaxpr/psum | solution.py:21
  98.1 5.7 %psum.49 = f32[1024]{0:T(1024)S(1)} all-reduce(f32[1024]{0:T(1024)S(1)} %get-tuple-element.759), channel_id=1, replica_groups=mesh['blk'=8,'rank'=4] {'rank'}, use_global_device_ids=true, to_apply=%region_6.0 | all-reduce | flops 1024 | bytes 8192 | tf_op jit(solution)/shard_map/while/body/eval_jaxpr/psum | solution.py:21
  111.0 6.2 %psum.49 = f32[1024]{0:T(1024)S(1)} all-reduce(f32[1024]{0:T(1024)S(1)} %get-tuple-element.759), channel_id=1, replica_groups=mesh['blk'=8,'rank'=4] {'rank'}, use_global_device_ids=true, to_apply=%region_6.0 | all-reduce | flops 1024 | bytes 8192 | tf_op jit(solution)/shard_map/while/body/eval_jaxpr/psum | solution.py:21
  121.5 10.2 %collective-permute-done.1 = f32[64,1024]{1,0:T(8,128)S(1)} collective-permute-done((f32[64,1024]{1,0:T(8,128)S(1)}, f32[64,1024]{1,0:T(8,128)S(1)}, u32[]{:S(2)}, u32[]{:S(2)}) %collective-permute-start.1) | collective-permute-done | bytes 262176 | tf_op jit(solution)/shard_map/ppermute | solution.py:17
  131.7 54.0 %while.62 = (s32[]{:T(128)}, f32[64,512]{1,0:T(8,128)S(1)}, f32[64,1024]{1,0:T(8,128)S(1)}, s32[]{:T(128)}, f32[4096]{0:T(1024)S(1)}, /*index=5*/s32[4096]{0:T(1...) while((s32[]{:T(128)}, f32[64,512]{1,0:T(8,128)S(1)}, ...), condition=%wide.region_11.0_spmd, body=%wide.region_8.0_spmd.sunk | while | flops 2419825664 | bytes 3092663 | solution.py:74
  135.0 5.7 %psum.50 = f32[1024]{0:T(1024)S(1)} all-reduce(f32[1024]{0:T(1024)S(1)} %get-tuple-element.768), channel_id=1, replica_groups=mesh['blk'=8,'rank'=4] {'rank'}, use_global_device_ids=true, to_apply=%region_10.0 | all-reduce | flops 1024 | bytes 8192 | tf_op jit(solution)/shard_map/while/body/eval_jaxpr/psum | solution.py:21
  148.1 6.2 %psum.50 = f32[1024]{0:T(1024)S(1)} all-reduce(f32[1024]{0:T(1024)S(1)} %get-tuple-element.768), channel_id=1, replica_groups=mesh['blk'=8,'rank'=4] {'rank'}, use_global_device_ids=true, to_apply=%region_10.0 | all-reduce | flops 1024 | bytes 8192 | tf_op jit(solution)/shard_map/while/body/eval_jaxpr/psum | solution.py:21
  161.8 5.7 %psum.50 = f32[1024]{0:T(1024)S(1)} all-reduce(f32[1024]{0:T(1024)S(1)} %get-tuple-element.768), channel_id=1, replica_groups=mesh['blk'=8,'rank'=4] {'rank'}, use_global_device_ids=true, to_apply=%region_10.0 | all-reduce | flops 1024 | bytes 8192 | tf_op jit(solution)/shard_map/while/body/eval_jaxpr/psum | solution.py:21
  175.0 6.6 %psum.50 = f32[1024]{0:T(1024)S(1)} all-reduce(f32[1024]{0:T(1024)S(1)} %get-tuple-element.768), channel_id=1, replica_groups=mesh['blk'=8,'rank'=4] {'rank'}, use_global_device_ids=true, to_apply=%region_10.0 | all-reduce | flops 1024 | bytes 8192 | tf_op jit(solution)/shard_map/while/body/eval_jaxpr/psum | solution.py:21
  185.8 9.9 %collective-permute-done.2 = f32[64,1024]{1,0:T(8,128)S(1)} collective-permute-done((f32[64,1024]{1,0:T(8,128)S(1)}, f32[64,1024]{1,0:T(8,128)S(1)}, u32[]{:S(2)}, u32[]{:S(2)}) %collective-permute-start.2) | collective-permute-done | bytes 262176 | tf_op jit(solution)/shard_map/ppermute | solution.py:17
  195.7 53.7 %while.63 = (s32[]{:T(128)}, f32[64,512]{1,0:T(8,128)S(1)}, f32[64,1024]{1,0:T(8,128)S(1)}, s32[]{:T(128)}, f32[4096]{0:T(1024)S(1)}, /*index=5*/s32[4096]{0:T(1...) while((s32[]{:T(128)}, f32[64,512]{1,0:T(8,128)S(1)}, ...), condition=%wide.region_15.0_spmd, body=%wide.region_12.0_spmd.sunk | while | flops 2419825664 | bytes 3092663 | solution.py:74
  198.9 5.7 %psum.51 = f32[1024]{0:T(1024)S(1)} all-reduce(f32[1024]{0:T(1024)S(1)} %get-tuple-element.777), channel_id=1, replica_groups=mesh['blk'=8,'rank'=4] {'rank'}, use_global_device_ids=true, to_apply=%region_14.0 | all-reduce | flops 1024 | bytes 8192 | tf_op jit(solution)/shard_map/while/body/eval_jaxpr/psum | solution.py:21
  211.9 6.6 %psum.51 = f32[1024]{0:T(1024)S(1)} all-reduce(f32[1024]{0:T(1024)S(1)} %get-tuple-element.777), channel_id=1, replica_groups=mesh['blk'=8,'rank'=4] {'rank'}, use_global_device_ids=true, to_apply=%region_14.0 | all-reduce | flops 1024 | bytes 8192 | tf_op jit(solution)/shard_map/while/body/eval_jaxpr/psum | solution.py:21
  225.9 5.7 %psum.51 = f32[1024]{0:T(1024)S(1)} all-reduce(f32[1024]{0:T(1024)S(1)} %get-tuple-element.777), channel_id=1, replica_groups=mesh['blk'=8,'rank'=4] {'rank'}, use_global_device_ids=true, to_apply=%region_14.0 | all-reduce | flops 1024 | bytes 8192 | tf_op jit(solution)/shard_map/while/body/eval_jaxpr/psum | solution.py:21
  239.0 6.2 %psum.51 = f32[1024]{0:T(1024)S(1)} all-reduce(f32[1024]{0:T(1024)S(1)} %get-tuple-element.777), channel_id=1, replica_groups=mesh['blk'=8,'rank'=4] {'rank'}, use_global_device_ids=true, to_apply=%region_14.0 | all-reduce | flops 1024 | bytes 8192 | tf_op jit(solution)/shard_map/while/body/eval_jaxpr/psum | solution.py:21
  249.5 8.4 %collective-permute-done.3 = f32[64,1024]{1,0:T(8,128)S(1)} collective-permute-done((f32[64,1024]{1,0:T(8,128)S(1)}, f32[64,1024]{1,0:T(8,128)S(1)}, u32[]{:S(2)}, u32[]{:S(2)}) %collective-permute-start.3) | collective-permute-done | bytes 262176 | tf_op jit(solution)/shard_map/ppermute | solution.py:17
  (151 shorter events, 120.8 us)
Async XLA Ops:
  0.6 0.7 copy-start.6
  0.6 1.3 copy-start.3
  0.7 1.4 copy-start.4
  0.7 1.4 copy-start.5
  0.7 1.5 copy-start
  0.7 1.5 copy-start.2
  57.2 11.1 %collective-permute-start = (f32[64,1024]{1,0:T(8,128)S(1)}, f32[64,1024]{1,0:T(8,128)S(1)}, u32[]{:S(2)}, u32[]{:S(2)}) collective-permute-start(f32[64,1024]{1,0:T(8,128)S(1)} %get-tuple-element.503), channel_id=1, source_target_pairs={{28,0},{0,4},{4,8},{8,12},{12,16},{16,20},{20,24},{24,28},{29,1},{... | collective-permute-start | bytes 786440 | tf_op jit(solution)/shard_map/ppermute | solution.py:17
  121.3 10.5 %collective-permute-start.1 = (f32[64,1024]{1,0:T(8,128)S(1)}, f32[64,1024]{1,0:T(8,128)S(1)}, u32[]{:S(2)}, u32[]{:S(2)}) collective-permute-start(f32[64,1024]{1,0:T(8,128)S(1)} %get-tuple-element.505), channel_id=1, source_target_pairs={{28,0},{0,4},{4,8},{8,12},{12,16},{16,20},{20,24},{24,28},{29,1},{... | collective-permute-start | bytes 786440 | tf_op jit(solution)/shard_map/ppermute | solution.py:17
  185.8 9.9 %collective-permute-start.2 = (f32[64,1024]{1,0:T(8,128)S(1)}, f32[64,1024]{1,0:T(8,128)S(1)}, u32[]{:S(2)}, u32[]{:S(2)}) collective-permute-start(f32[64,1024]{1,0:T(8,128)S(1)} %get-tuple-element.507), channel_id=1, source_target_pairs={{28,0},{0,4},{4,8},{8,12},{12,16},{16,20},{20,24},{24,28},{29,1},{... | collective-permute-start | bytes 786440 | tf_op jit(solution)/shard_map/ppermute | solution.py:17
  249.4 9.2 %copy-start.1 = (f32[64,512]{1,0:T(8,128)}, f32[64,512]{1,0:T(8,128)S(1)}, u32[]{:S(2)}) copy-start(f32[64,512]{1,0:T(8,128)S(1)} %get-tuple-element.912) | copy-start | bytes 393220
  249.4 8.5 %collective-permute-start.3 = (f32[64,1024]{1,0:T(8,128)S(1)}, f32[64,1024]{1,0:T(8,128)S(1)}, u32[]{:S(2)}, u32[]{:S(2)}) collective-permute-start(f32[64,1024]{1,0:T(8,128)S(1)} %get-tuple-element.509), channel_id=1, source_target_pairs={{12,0},{16,4},{20,8},{24,12},{28,16},{0,20},{4,24},{8,28},{13,1},{... | collective-permute-start | bytes 786440 | tf_op jit(solution)/shard_map/ppermute | solution.py:17
where the time goes:
time: 259 us
  blocking collectives  97.9 us (38%)
  matrix products  96 us (37%)
  waiting for transfers between devices  37.9 us (15%)
  other arithmetic  20.4 us (8%)
    psum x16, blocking collectives, rank_total(): return lax.psum(partial_values, 'rank')  97.9 us
    dot_general x32, matrix products, spread_columns(): lax.dot_general(steps, chooser, (((1,), (1,)), ((), ())), preferred_eleme...  56 us
    dot_general x32, matrix products, pick_columns(): jnp.dot(block, chooser, preferred_element_type=jnp.float32, precision=lax...  40 us
    ppermute x4, waiting for transfers between devices, shifted(): return lax.ppermute(block, axis, route)  37.9 us
    mul x16, other arithmetic, update(): errors = weights * (targets - predicted)  10.2 us
    mul x16, other arithmetic, update(): DECAY_WEIGHT * weights[None, :] * user_vecs  10.2 us
  transfers between devices with their start and end apart: 4, of which 4 were waited for; matrix products, arithmetic and copies ran while one was open for 0% of the time, Pallas kernels for 0%

commit v1 on v0

v1 whole, which is shorter than its diff:
```python
import functools

import jax
import jax.numpy as jnp
from jax import lax
from jax.experimental import pallas as pl
from jax.experimental.pallas import tpu as pltpu
from jax.sharding import PartitionSpec as P

BATCH = 1024
LANES = 128
GROUPS = BATCH // LANES
CHUNK = 256
LEARN_RATE = 0.05
DECAY_WEIGHT = 0.02
MESH = pl.DeviceIdType.MESH


def split_rows(block):
    high = block.astype(jnp.bfloat16)
    low = (block - high.astype(jnp.float32)).astype(jnp.bfloat16)
    return high, low


def kernel(
    blocks, ranks,
    u_in, v_in, rows, cols, vals, count,
    u_out, v_out,
    users, u_cat, v_cat, held, tiles, chooser, u_pick, v_pick, u_step, v_step,
    partial, arrived, errs,
    part_send, part_recv, tile_send, tile_recv, user_send, user_recv,
):
    depth, user_count = u_in.shape
    item_count = v_in.shape[1]
    strata = rows.shape[1]
    tile = rows.shape[2]
    per_tile = tile // BATCH
    spans = tile // LANES
    batches = strata * per_tile
    blk = lax.axis_index("blk")
    rank = lax.axis_index("rank")

    def at_blk(shift):
        return (lax.rem(blk + (shift % blocks), blocks), rank)

    def at_rank(shift):
        return (blk, lax.rem(rank + (shift % ranks), ranks))

    barrier = pltpu.get_barrier_semaphore()
    met = [at_rank(o) for o in range(1, ranks)]
    met += [at_blk(o) for o in range(1, strata)] + [at_blk(-o) for o in range(1, strata)]
    for device in met:
        pl.semaphore_signal(barrier, inc=1, device_id=device, device_id_type=MESH)

    stratum_at = lax.broadcasted_iota(jnp.int32, (strata, LANES), 0)
    lane_at = lax.broadcasted_iota(jnp.int32, (strata, LANES), 1)
    live = jnp.zeros((strata, LANES), jnp.int32)
    for s in range(strata):
        live = jnp.where(stratum_at == s, count[0, s], live)
    for r in range(spans):
        here = slice(r * LANES, (r + 1) * LANES)
        alive = lane_at + r * LANES < live
        held[:, r, :] = jnp.where(alive, rows[0, :, here], -1).astype(jnp.float32)
        held[:, spans + r, :] = jnp.where(alive, cols[0, :, here], -1).astype(jnp.float32)
        held[:, 2 * spans + r, :] = vals[0, :, here]
    tiles[0] = held[0]

    def build(slot, s, q):
        at = pl.multiple_of(q * GROUPS, GROUPS)
        for base, size, first in ((0, user_count, 0), (user_count, item_count, spans)):
            index = tiles[s, pl.ds(first + at, GROUPS), :].astype(jnp.int32)
            for j in range(GROUPS):
                row = index[j : j + 1, :]
                for t in range(0, size, CHUNK):
                    place = lax.broadcasted_iota(jnp.int32, (CHUNK, LANES), 0) + t
                    chooser[slot, base + t : base + t + CHUNK, j * LANES : (j + 1) * LANES] = (
                        jnp.where(place == row, 1.0, 0.0).astype(jnp.bfloat16)
                    )

    def cut_users(s):
        high, low = split_rows(users[s])
        u_cat[:depth] = high
        u_cat[depth:] = low

    users[0] = u_in[...]
    v_out[...] = v_in[...]
    cut_users(0)
    high, low = split_rows(v_in[...])
    v_cat[:depth] = high
    v_cat[depth:] = low
    build(0, 0, 0)

    pl.semaphore_wait(barrier, len(met))

    def tile_copy(s):
        return pltpu.make_async_remote_copy(
            src_ref=held.at[s], dst_ref=tiles.at[s],
            send_sem=tile_send.at[s], recv_sem=tile_recv.at[s],
            device_id=(lax.rem(blk + blocks - s, blocks), rank),
            device_id_type=MESH,
        )

    for s in range(1, strata):
        tile_copy(s).start()

    def user_copy(s):
        return pltpu.make_async_remote_copy(
            src_ref=users.at[s], dst_ref=users.at[s + 1],
            send_sem=user_send.at[s], recv_sem=user_recv.at[s],
            device_id=at_blk(-1), device_id_type=MESH,
        )

    def part_copy(slot, o):
        return pltpu.make_async_remote_copy(
            src_ref=partial.at[slot], dst_ref=arrived.at[slot, o - 1],
            send_sem=part_send.at[slot, o - 1], recv_sem=part_recv.at[slot, o - 1],
            device_id=at_rank(o), device_id_type=MESH,
        )

    group_at = lax.broadcasted_iota(jnp.int32, (GROUPS, LANES), 0)

    @pl.loop(0, batches)
    def _(k):
        s = k // per_tile
        q = k % per_tile
        slot = k % 2
        total = jnp.zeros((GROUPS, LANES), jnp.float32)
        for c in range(0, BATCH, CHUNK):
            here = slice(c, c + CHUNK)
            u = jnp.dot(u_cat[...], chooser[slot, :user_count, here], preferred_element_type=jnp.float32)
            v = jnp.dot(v_cat[...], chooser[slot, user_count:, here], preferred_element_type=jnp.float32)
            u = u[:depth] + u[depth:]
            v = v[:depth] + v[depth:]
            u_pick[:, here] = u
            v_pick[:, here] = v
            sums = jnp.sum(u * v, axis=0, keepdims=True)
            for h in range(0, CHUNK, LANES):
                total = jnp.where(group_at == (c + h) // LANES, sums[:, h : h + LANES], total)
        partial[slot] = total
        for o in range(1, ranks):
            part_copy(slot, o).start()

        @pl.when(jnp.logical_and(q == per_tile - 1, s < strata - 1))
        def _():
            tile_copy(s + 1).wait_recv()

        @pl.when(k < batches - 1)
        def _():
            build((k + 1) % 2, (k + 1) // per_tile, (k + 1) % per_tile)

        for o in range(1, ranks):
            part_copy(slot, o).wait()
            total = total + arrived[slot, o - 1]
        at = pl.multiple_of(2 * spans + q * GROUPS, GROUPS)
        errs[...] = tiles[s, pl.ds(at, GROUPS), :] - total
        for j in range(GROUPS):
            here = slice(j * LANES, (j + 1) * LANES)
            e = errs[j : j + 1, :]
            u = u_pick[:, here]
            v = v_pick[:, here]
            high, low = split_rows(LEARN_RATE * (e * v - DECAY_WEIGHT * u))
            u_step[:depth, here] = high
            u_step[depth:, here] = low
            high, low = split_rows(LEARN_RATE * (e * u - DECAY_WEIGHT * v))
            v_step[:depth, here] = high
            v_step[depth:, here] = low

        def spread(steps, first):
            moved = lax.dot_general(
                steps[...], chooser[slot, first : first + CHUNK, :],
                (((1,), (1,)), ((), ())), preferred_element_type=jnp.float32,
            )
            return moved[:depth] + moved[depth:]

        for t in range(0, user_count, CHUNK):
            here = slice(t, t + CHUNK)
            new = users[s, :, here] + spread(u_step, t)
            users[s, :, here] = new
            high, low = split_rows(new)
            u_cat[:depth, here] = high
            u_cat[depth:, here] = low
        turn = jnp.logical_and(q == per_tile - 1, s < strata - 1)

        @pl.when(turn)
        def _():
            user_copy(s).start()

        for t in range(0, item_count, CHUNK):
            here = slice(t, t + CHUNK)
            new = v_out[:, here] + spread(v_step, user_count + t)
            v_out[:, here] = new
            high, low = split_rows(new)
            v_cat[:depth, here] = high
            v_cat[depth:, here] = low

        @pl.when(turn)
        def _():
            user_copy(s).wait()
            cut_users(s + 1)

    home = pltpu.make_async_remote_copy(
        src_ref=users.at[strata - 1], dst_ref=u_out,
        send_sem=user_send.at[strata - 1], recv_sem=user_recv.at[strata - 1],
        device_id=at_blk(strata - 1), device_id_type=MESH,
    )
    home.start()
    for s in range(1, strata):
        tile_copy(s).wait_send()
    home.wait()


def solution(mesh):
    blocks, ranks = mesh.shape["blk"], mesh.shape["rank"]

    def per_device(user_factors, item_factors, tile_rows, tile_cols, tile_vals, tile_count):
        depth, user_count = user_factors.shape
        item_count = item_factors.shape[1]
        strata, tile = tile_rows.shape[1:]
        held = (strata, 3 * tile // LANES, LANES)
        vmem = pl.BlockSpec(memory_space=pltpu.VMEM)
        f32, bf16 = jnp.float32, jnp.bfloat16
        return pl.pallas_call(
            functools.partial(kernel, blocks, ranks),
            out_shape=(
                jax.ShapeDtypeStruct((depth, user_count), f32),
                jax.ShapeDtypeStruct((depth, item_count), f32),
            ),
            in_specs=[vmem] * 5 + [pl.BlockSpec(memory_space=pltpu.SMEM)],
            out_specs=(vmem, vmem),
            scratch_shapes=[
                pltpu.VMEM((strata, depth, user_count), f32),
                pltpu.VMEM((2 * depth, user_count), bf16),
                pltpu.VMEM((2 * depth, item_count), bf16),
                pltpu.VMEM(held, f32),
                pltpu.VMEM(held, f32),
                pltpu.VMEM((2, user_count + item_count, BATCH), bf16),
                pltpu.VMEM((depth, BATCH), f32),
                pltpu.VMEM((depth, BATCH), f32),
                pltpu.VMEM((2 * depth, BATCH), bf16),
                pltpu.VMEM((2 * depth, BATCH), bf16),
                pltpu.VMEM((2, GROUPS, LANES), f32),
                pltpu.VMEM((2, ranks - 1, GROUPS, LANES), f32),
                pltpu.VMEM((GROUPS, LANES), f32),
                pltpu.SemaphoreType.DMA((2, ranks - 1)),
                pltpu.SemaphoreType.DMA((2, ranks - 1)),
                pltpu.SemaphoreType.DMA((strata,)),
                pltpu.SemaphoreType.DMA((strata,)),
                pltpu.SemaphoreType.DMA((strata,)),
                pltpu.SemaphoreType.DMA((strata,)),
            ],
            compiler_params=pltpu.CompilerParams(
                collective_id=0, has_side_effects=True, vmem_limit_bytes=32 * 1024 * 1024
            ),
        )(user_factors, item_factors, tile_rows, tile_cols, tile_vals, tile_count)

    placed = (
        P("rank", "blk"),
        P("rank", "blk"),
        P("blk", None, None),
        P("blk", None, None),
        P("blk", None, None),
        P("blk", None),
    )
    return jax.shard_map(
        per_device,
        mesh=mesh,
        in_specs=placed,
        out_specs=(P("rank", "blk"), P("rank", "blk")),
        check_vma=False,
    )
```

time: 259 us -> 111 us (0.43)
  Pallas kernels: 0 us -> 104 us
  blocking collectives: 97.9 us -> 0 us
  matrix products: 96 us -> 0 us
  waiting for transfers between devices: 37.9 us -> 0 us
  other arithmetic: 20.4 us -> 0 us
  local copies, waits for them, and re-layouts: 2.42 us -> 6.38 us
    pallas_call x0 -> x1, Pallas kernels: none -> 104 us  [per_device(): pl.pallas_call(functools.partial(kernel, blocks, ranks), out_shape=(jax.S...]
    psum x16 -> x0, blocking collectives: 97.9 us -> none  [rank_total(): return lax.psum(partial_values, 'rank')]
    dot_general x64 -> x0, matrix products: 96 us -> none  [the longest x32 56 us: spread_columns(): lax.dot_general(steps, chooser, (((1,), (1,)), ((), ())), preferred_eleme...]
    ppermute x4 -> x0, waiting for transfers between devices: 37.9 us -> none  [shifted(): return lax.ppermute(block, axis, route)]
    mul x32 -> x0, other arithmetic: 20.4 us -> none  [the longest x16 10.2 us: update(): errors = weights * (targets - predicted)]
    unnamed x15 -> x14, local copies, waits for them, and re-layouts: 1.33 us -> 6.38 us
  transfers between devices with their start and end apart: 4 -> 0, of which waited for: 4 -> 0; matrix products, arithmetic and copies ran while one was open for 0% -> 0% of each run, Pallas kernels for 0% -> 0%
where the time goes in v1:
time: 111 us
  Pallas kernels  104 us (94%)
  local copies, waits for them, and re-layouts  6.38 us (6%)
    pallas_call x1, Pallas kernels, per_device(): pl.pallas_call(functools.partial(kernel, blocks, ranks), out_shape=(jax.S...  104 us
    unnamed x14, local copies, waits for them, and re-layouts  6.38 us

profile of v1, /device:TPU:0, one launch (start us, length us, event | category | flops | bytes accessed | tf_op | source)
XLA Modules:
  0.0 111.0 jit_solution(1584118671878565483)
XLA Ops:
  0.6 0.0 copy-start
  0.6 0.9 copy-done
  1.6 0.0 copy-start.1
  1.6 0.9 copy-done.1
  2.5 0.0 copy-start.2
  2.5 0.8 copy-done.2
  3.3 0.0 copy-start.3
  3.3 0.8 copy-done.3
  4.2 0.0 copy-start.4
  4.2 0.8 copy-done.4
  5.0 0.0 copy-start.5
  5.0 0.7 copy-done.5
  5.7 103.9 %shard_map.77 = (f32[64,512]{1,0:T(8,128)S(1)}, f32[64,1024]{1,0:T(8,128)S(1)}) custom-call(f32[64,512]{1,0:T(8,128)S(1)} %copy-done.1, f32[64,1024]{1,0:T(8,128)S(1)} %copy-done, s32[1,4,4096]{2,1,0:T(4,128)S(1)} %copy-done.2, s32[1,4,4096]{2,1,0:T(4,128)S(1)} %copy-done.3, f32[1,4,4096]{2,1,0:T(4,128)S(1)} %copy-done.4, s32[1,4]{1,0:T(1,128)S(1)} %copy-done.5), custom_call_target="tpu_custom_call" | custom-call | tf_op jit(solution)/shard_map/pallas_call | solution.py:222
  109.6 0.7 copy.10
  110.3 0.7 copy.11
Async XLA Ops:
  0.6 1.0 copy-start
  1.6 0.9 copy-start.1
  2.5 0.8 copy-start.2
  3.3 0.8 copy-start.3
  4.2 0.8 copy-start.4
  5.0 0.7 copy-start.5

commit v2 on v1

v2 whole, which is shorter than its diff:
```python
import functools

import jax
import jax.numpy as jnp
from jax import lax
from jax.experimental import pallas as pl
from jax.experimental.pallas import tpu as pltpu
from jax.sharding import PartitionSpec as P

BATCH = 1024
LANES = 128
GROUPS = BATCH // LANES
CHUNK = 256
HALVES = 1
HALF = BATCH // HALVES
HALF_GROUPS = GROUPS // HALVES
LEARN_RATE = 0.05
DECAY_WEIGHT = 0.02
MESH = pl.DeviceIdType.MESH


def split_rows(block):
    high = block.astype(jnp.bfloat16)
    low = (block - high.astype(jnp.float32)).astype(jnp.bfloat16)
    return high, low


def kernel(
    blocks, ranks,
    u_in, v_in, rows_in, cols_in, vals_in, count_in,
    u_out, v_out,
    rows, cols, vals, count, users, u_cat, v_cat, held, tiles, chooser, spreader, u_pick, v_pick, u_step, v_step,
    partial, arrived, errs,
    part_send, part_recv, tile_send, tile_recv, user_send, user_recv, load_sem,
):
    depth, user_count = u_in.shape
    item_count = v_in.shape[1]
    strata, tile = rows_in.shape[1:]
    per_tile = tile // BATCH
    spans = tile // LANES
    batches = strata * per_tile
    blk = lax.axis_index("blk")
    rank = lax.axis_index("rank")

    def at_blk(shift):
        return (lax.rem(blk + (shift % blocks), blocks), rank)

    def at_rank(shift):
        return (blk, lax.rem(rank + (shift % ranks), ranks))

    barrier = pltpu.get_barrier_semaphore()
    met = [at_rank(o) for o in range(1, ranks)]
    met += [at_blk(o) for o in range(1, strata)] + [at_blk(-o) for o in range(1, strata)]
    for device in met:
        pl.semaphore_signal(barrier, inc=1, device_id=device, device_id_type=MESH)

    loads = [
        pltpu.make_async_copy(source, target, load_sem.at[i])
        for i, (source, target) in enumerate(
            (
                (count_in, count), (rows_in, rows), (cols_in, cols), (vals_in, vals),
                (u_in, users.at[0]), (v_in, v_out),
            )
        )
    ]
    for load in loads:
        load.start()
    for load in loads[:4]:
        load.wait()

    stratum_at = lax.broadcasted_iota(jnp.int32, (strata, LANES), 0)
    lane_at = lax.broadcasted_iota(jnp.int32, (strata, LANES), 1)
    live = jnp.zeros((strata, LANES), jnp.int32)
    for s in range(strata):
        live = jnp.where(stratum_at == s, count[0, s], live)
    for r in range(spans):
        here = slice(r * LANES, (r + 1) * LANES)
        alive = lane_at + r * LANES < live
        held[:, r, :] = jnp.where(alive, rows[0, :, here], -1).astype(jnp.float32)
        held[:, spans + r, :] = jnp.where(alive, cols[0, :, here], -1).astype(jnp.float32)
        held[:, 2 * spans + r, :] = vals[0, :, here]
    tiles[0] = held[0]

    parts = ((0, user_count, 0), (user_count, item_count, spans))
    down = lax.broadcasted_iota(jnp.int32, (CHUNK, LANES), 0)
    across = lax.broadcasted_iota(jnp.int32, (LANES, LANES), 1)

    def chosen(place, index):
        return jnp.where(place == index, 1.0, 0.0).astype(jnp.bfloat16)

    def index_of(s, q, first):
        at = pl.multiple_of(first + q * GROUPS, GROUPS)
        return tiles[s, pl.ds(at, GROUPS), :].astype(jnp.int32)

    def build_chooser(s, q):
        for base, size, first in parts:
            index = index_of(s, q, first)
            for j in range(GROUPS):
                row = jnp.broadcast_to(index[j : j + 1, :], (CHUNK, LANES))
                for t in range(0, size, CHUNK):
                    chooser[base + t : base + t + CHUNK, j * LANES : (j + 1) * LANES] = (
                        chosen(down + t, row)
                    )

    def build_spreader(s, q):
        for base, size, first in parts:
            index = jnp.transpose(index_of(s, q, first))
            for j in range(GROUPS):
                column = jnp.broadcast_to(index[:, j : j + 1], (LANES, LANES))
                for t in range(0, size, LANES):
                    spreader[j * LANES : (j + 1) * LANES, base + t : base + t + LANES] = (
                        chosen(across + t, column)
                    )

    def cut_users(s):
        high, low = split_rows(users[s])
        u_cat[:depth] = high
        u_cat[depth:] = low

    build_chooser(0, 0)
    for load in loads[4:]:
        load.wait()
    cut_users(0)
    high, low = split_rows(v_out[...])
    v_cat[:depth] = high
    v_cat[depth:] = low

    def tile_copy(s):
        return pltpu.make_async_remote_copy(
            src_ref=held.at[s], dst_ref=tiles.at[s],
            send_sem=tile_send.at[s], recv_sem=tile_recv.at[s],
            device_id=(lax.rem(blk + blocks - s, blocks), rank),
            device_id_type=MESH,
        )

    def user_copy(s):
        return pltpu.make_async_remote_copy(
            src_ref=users.at[s], dst_ref=users.at[s + 1],
            send_sem=user_send.at[s], recv_sem=user_recv.at[s],
            device_id=at_blk(-1), device_id_type=MESH,
        )

    def home():
        return pltpu.make_async_remote_copy(
            src_ref=users.at[strata - 1], dst_ref=u_out,
            send_sem=user_send.at[strata - 1], recv_sem=user_recv.at[strata - 1],
            device_id=at_blk(strata - 1), device_id_type=MESH,
        )

    def part_copy(slot, h, o):
        return pltpu.make_async_remote_copy(
            src_ref=partial.at[slot, h], dst_ref=arrived.at[slot, h, o - 1],
            send_sem=part_send.at[slot, h, o - 1], recv_sem=part_recv.at[slot, h, o - 1],
            device_id=at_rank(o), device_id_type=MESH,
        )

    group_at = lax.broadcasted_iota(jnp.int32, (HALF_GROUPS, LANES), 0)

    @pl.loop(0, batches)
    def _(k):
        s = k // per_tile
        q = k % per_tile
        slot = k % 2
        totals = []
        for h in range(HALVES):
            total = jnp.zeros((HALF_GROUPS, LANES), jnp.float32)
            for c in range(h * HALF, (h + 1) * HALF, CHUNK):
                here = slice(c, c + CHUNK)
                u = jnp.dot(u_cat[...], chooser[:user_count, here], preferred_element_type=jnp.float32)
                u = u[:depth] + u[depth:]
                v = jnp.dot(v_cat[...], chooser[user_count:, here], preferred_element_type=jnp.float32)
                v = v[:depth] + v[depth:]
                u_pick[:, here] = u
                v_pick[:, here] = v
                sums = jnp.sum(u * v, axis=0, keepdims=True)
                for g in range(0, CHUNK, LANES):
                    total = jnp.where(
                        group_at == (c - h * HALF + g) // LANES, sums[:, g : g + LANES], total
                    )
            partial[slot, h] = total
            if h == 0:

                @pl.when(k == 0)
                def _():
                    pl.semaphore_wait(barrier, len(met))

            for o in range(1, ranks):
                part_copy(slot, h, o).start()
            totals.append(total)
        turn = jnp.logical_and(q == per_tile - 1, s < strata - 1)

        @pl.when(k == 0)
        def _():
            for other in range(1, strata):
                tile_copy(other).start()

        build_spreader(s, q)

        @pl.when(turn)
        def _():
            tile_copy(s + 1).wait_recv()

        @pl.when(k < batches - 1)
        def _():
            build_chooser((k + 1) // per_tile, (k + 1) % per_tile)

        for h in range(HALVES):
            total = totals[h]
            for o in range(1, ranks):
                part_copy(slot, h, o).wait()
                total = total + arrived[slot, h, o - 1]
            at = pl.multiple_of(2 * spans + q * GROUPS, GROUPS)
            targets = tiles[s, pl.ds(at, GROUPS), :]
            errs[h] = targets[h * HALF_GROUPS : (h + 1) * HALF_GROUPS] - total
            for j in range(HALF_GROUPS):
                here = slice(h * HALF + j * LANES, h * HALF + (j + 1) * LANES)
                e = errs[h, j : j + 1, :]
                u = u_pick[:, here]
                v = v_pick[:, here]
                high, low = split_rows(LEARN_RATE * (e * v - DECAY_WEIGHT * u))
                u_step[:depth, here] = high
                u_step[depth:, here] = low
                high, low = split_rows(LEARN_RATE * (e * u - DECAY_WEIGHT * v))
                v_step[:depth, here] = high
                v_step[depth:, here] = low
            span = slice(h * HALF, (h + 1) * HALF)
            last = h == HALVES - 1

            def spread(steps, first):
                moved = jnp.dot(
                    steps[:, span], spreader[span, first : first + CHUNK],
                    preferred_element_type=jnp.float32,
                )
                return moved[:depth] + moved[depth:]

            for t in range(0, user_count, CHUNK):
                here = slice(t, t + CHUNK)
                new = users[s, :, here] + spread(u_step, t)
                users[s, :, here] = new
                if last:
                    high, low = split_rows(new)
                    u_cat[:depth, here] = high
                    u_cat[depth:, here] = low
            if last:

                @pl.when(turn)
                def _():
                    user_copy(s).start()

                @pl.when(k == batches - 1)
                def _():
                    home().start()

            for t in range(0, item_count, CHUNK):
                here = slice(t, t + CHUNK)
                new = v_out[:, here] + spread(v_step, user_count + t)
                v_out[:, here] = new
                if last:
                    high, low = split_rows(new)
                    v_cat[:depth, here] = high
                    v_cat[depth:, here] = low

        @pl.when(turn)
        def _():
            user_copy(s).wait()
            cut_users(s + 1)

    for s in range(1, strata):
        tile_copy(s).wait_send()
    home().wait()


def solution(mesh):
    blocks, ranks = mesh.shape["blk"], mesh.shape["rank"]

    def per_device(user_factors, item_factors, tile_rows, tile_cols, tile_vals, tile_count):
        depth, user_count = user_factors.shape
        item_count = item_factors.shape[1]
        strata, tile = tile_rows.shape[1:]
        held = (strata, 3 * tile // LANES, LANES)
        vmem = pl.BlockSpec(memory_space=pltpu.VMEM)
        f32, bf16 = jnp.float32, jnp.bfloat16
        return pl.pallas_call(
            functools.partial(kernel, blocks, ranks),
            out_shape=(
                jax.ShapeDtypeStruct((depth, user_count), f32),
                jax.ShapeDtypeStruct((depth, item_count), f32),
            ),
            in_specs=[pl.BlockSpec(memory_space=pl.ANY)] * 6,
            out_specs=(vmem, vmem),
            scratch_shapes=[
                pltpu.VMEM(tile_rows.shape, jnp.int32),
                pltpu.VMEM(tile_cols.shape, jnp.int32),
                pltpu.VMEM(tile_vals.shape, f32),
                pltpu.SMEM(tile_count.shape, jnp.int32),
                pltpu.VMEM((strata, depth, user_count), f32),
                pltpu.VMEM((2 * depth, user_count), bf16),
                pltpu.VMEM((2 * depth, item_count), bf16),
                pltpu.VMEM(held, f32),
                pltpu.VMEM(held, f32),
                pltpu.VMEM((user_count + item_count, BATCH), bf16),
                pltpu.VMEM((BATCH, user_count + item_count), bf16),
                pltpu.VMEM((depth, BATCH), f32),
                pltpu.VMEM((depth, BATCH), f32),
                pltpu.VMEM((2 * depth, BATCH), bf16),
                pltpu.VMEM((2 * depth, BATCH), bf16),
                pltpu.VMEM((2, HALVES, HALF_GROUPS, LANES), f32),
                pltpu.VMEM((2, HALVES, ranks - 1, HALF_GROUPS, LANES), f32),
                pltpu.VMEM((HALVES, HALF_GROUPS, LANES), f32),
                pltpu.SemaphoreType.DMA((2, HALVES, ranks - 1)),
                pltpu.SemaphoreType.DMA((2, HALVES, ranks - 1)),
                pltpu.SemaphoreType.DMA((strata,)),
                pltpu.SemaphoreType.DMA((strata,)),
                pltpu.SemaphoreType.DMA((strata,)),
                pltpu.SemaphoreType.DMA((strata,)),
                pltpu.SemaphoreType.DMA((6,)),
            ],
            compiler_params=pltpu.CompilerParams(
                collective_id=0, has_side_effects=True, vmem_limit_bytes=60 * 1024 * 1024
            ),
        )(user_factors, item_factors, tile_rows, tile_cols, tile_vals, tile_count)

    placed = (
        P("rank", "blk"),
        P("rank", "blk"),
        P("blk", None, None),
        P("blk", None, None),
        P("blk", None, None),
        P("blk", None),
    )
    return jax.shard_map(
        per_device,
        mesh=mesh,
        in_specs=placed,
        out_specs=(P("rank", "blk"), P("rank", "blk")),
        check_vma=False,
    )
```

time: 111 us -> 97.2 us (0.88)
  Pallas kernels: 104 us -> 94.1 us
  local copies, waits for them, and re-layouts: 6.38 us -> 2.32 us
    pallas_call x1, Pallas kernels: 104 us -> 94.1 us  [per_device(): pl.pallas_call(functools.partial(kernel, blocks, ranks), out_shape=(jax.S...]
    unnamed x14 -> x4, local copies, waits for them, and re-layouts: 6.38 us -> 2.32 us
where the time goes in v2:
time: 97.2 us; the launch traced here: 97.1 us
  Pallas kernels  94.1 us (97%)
  local copies, waits for them, and re-layouts  2.32 us (2%)
    pallas_call x1, Pallas kernels, per_device(): pl.pallas_call(functools.partial(kernel, blocks, ranks), out_shape=(jax.S...  94.1 us
    unnamed x4, local copies, waits for them, and re-layouts  2.32 us

profile of v2, /device:TPU:0, one launch (start us, length us, event | category | flops | bytes accessed | tf_op | source)
XLA Modules:
  0.0 97.1 jit_solution(8903558266047173539)
XLA Ops:
  0.6 94.1 %shard_map.77 = (f32[64,512]{1,0:T(8,128)}, f32[64,1024]{1,0:T(8,128)}) custom-call(f32[64,512]{1,0:T(8,128)} %u_in.1, f32[64,1024]{1,0:T(8,128)} %v_in.1, s32[1,4,4096]{2,1,0:T(4,128)} %rows_in.1, s32[1,4,4096]{2,1,0:T(4,128)} %cols_in.1, f32[1,4,4096]{2,1,0:T(4,128)} %vals_in.1, s32[1,4]{1,0:T(1,128)} %count_in.1), custom_call_target="tpu_custom_call" | custom-call | tf_op jit(solution)/shard_map/pallas_call | solution.py:283
  94.8 0.0 copy-start
  94.8 1.6 %copy.10 = f32[64,512]{1,0:T(8,128)} copy(f32[64,512]{1,0:T(8,128)} %get-tuple-element.4) | data formatting | bytes 262144
  96.4 0.0 copy-done
  96.4 0.7 copy.11
Async XLA Ops:
  94.8 1.6 %copy-start = (f32[64,1024]{1,0:T(8,128)S(1)}, f32[64,1024]{1,0:T(8,128)}, u32[]{:S(2)}) copy-start(f32[64,1024]{1,0:T(8,128)} %get-tuple-element.5) | copy-start | bytes 786436
